TPU v7x, 512 devices: a whole 4x4x16 slice. The times are simulated.
512 devices in a mesh: expert: 8 (over z_lo), etp: 32 (over x, y, z_hi), dp: 2 (over core).
Axes of the slice: x: 4, y: 4, z: 16 (z_hi: 2, z_lo: 8; z = z_hi * 8 + z_lo), core: 2. Of those that a mesh axis runs over, the one named last changes fastest.
Arguments:
- out_grad: bfloat16 [4096, 3072], P(('expert', 'etp', 'dp')), may hold values from -0.59765625 to 0.59765625
- routes: int32 [4096, 2], P(('expert', 'etp', 'dp')), may hold values from 0 to 7, all different within a row; in each aligned block of 8 rows (0 to 7, 8 to 15, ...) at most 4 rows name the same one
- route_weight: bfloat16 [4096, 2], P(('expert', 'etp', 'dp')), may hold values from 0.099609375 to 1
- saved_act: bfloat16 [2, 2, 8, 1024, 8192], P(None, 'dp', 'expert', None, 'etp'), may hold values from -6 to 6
- w_down: bfloat16 [8, 8192, 3072], P('expert', 'etp'), may hold values from -0.109375 to 0.109375
Outputs:
- d_act: bfloat16 [2, 2, 8, 1024, 8192], P(None, 'dp', 'expert', None, 'etp')
- d_weight: bfloat16 [8, 8192, 3072], P('expert', 'etp', 'dp')
- d_route: float32 [4096, 2], P(('expert', 'etp', 'dp'))
Inputs may be any that keep to these rules, and one draw needn't show every extreme that they name: `routes`: A token's two experts differ. Among the 8 tokens of one device (an aligned block of rows) no expert is named more than 4 times, and in every draw some device names some expert exactly 4 times.
All inputs are finite; a program needn't handle non-finite values.
Results may differ from a plain program's by a relative error of at most 0.0049.
Values may be sent and summed in bfloat16 or wider, within the bound.
A program may use at most 64 MiB of HBM per device.

v0:
```python
import jax
import jax.numpy as jnp
from jax import lax
from jax.sharding import PartitionSpec as P


def slot_table(route_block, expert_count, capacity):
    flat_routes = route_block.reshape(-1)
    one_hot = (flat_routes[:, None] == jnp.arange(expert_count, dtype=jnp.int32)[None, :]).astype(
        jnp.int32
    )
    slot_rank = jnp.sum((jnp.cumsum(one_hot, axis=0) - one_hot) * one_hot, axis=1)
    match_expert = (
        flat_routes[None, None, :] == jnp.arange(expert_count, dtype=jnp.int32)[:, None, None]
    )
    match_slot = slot_rank[None, None, :] == jnp.arange(capacity, dtype=jnp.int32)[None, :, None]
    return jnp.logical_and(match_expert, match_slot).astype(jnp.float32)


def per_device(out_grad, routes, route_weight, saved_act, w_down):
    expert_count = lax.axis_size("expert")
    etp_count = lax.axis_size("etp")
    row_total = saved_act.shape[3]
    capacity = row_total // (expert_count * etp_count)
    tok_count = out_grad.shape[0]
    width = out_grad.shape[1]
    weight_mat = w_down[0]
    gate_pre = saved_act[0, 0, 0].astype(jnp.float32)
    up_pre = saved_act[1, 0, 0].astype(jnp.float32)
    gate_sig = jax.nn.sigmoid(gate_pre)
    hidden = gate_pre * gate_sig * up_pre
    own_table = slot_table(routes, expert_count, capacity)
    repeated = jnp.repeat(out_grad, 2, axis=0)
    outgoing = jnp.einsum(
        "ecj,jd->ecd", own_table.astype(jnp.bfloat16), repeated, preferred_element_type=jnp.float32
    ).astype(jnp.bfloat16)
    outgoing_weight = jnp.einsum(
        "ecj,j->ec",
        own_table,
        route_weight.reshape(-1).astype(jnp.float32),
        precision=lax.Precision.HIGHEST,
    ).astype(jnp.bfloat16)
    received, received_weight = (
        lax.all_to_all(
            outgoing.reshape(expert_count * capacity, width),
            "expert",
            split_axis=0,
            concat_axis=0,
            tiled=True,
        ),
        lax.all_to_all(
            outgoing_weight.reshape(expert_count * capacity),
            "expert",
            split_axis=0,
            concat_axis=0,
            tiled=True,
        ),
    )
    piece_rows = lax.all_gather(received, "etp", axis=0, tiled=True)
    piece_weight = lax.all_gather(received_weight, "etp", axis=0, tiled=True)
    row_weight = piece_weight.astype(jnp.float32)
    weighted = (row_weight[:, None] * hidden).astype(jnp.bfloat16)
    grad_part = lax.dot_general(
        weighted, piece_rows, (((0,), (0,)), ((), ())), preferred_element_type=jnp.float32
    )
    d_piece = lax.dot_general(
        piece_rows, weight_mat, (((1,), (1,)), ((), ())), preferred_element_type=jnp.float32
    )
    d_hidden = row_weight[:, None] * d_piece
    d_gate = (d_hidden * up_pre * gate_sig * (1.0 + gate_pre * (1.0 - gate_sig))).astype(
        jnp.bfloat16
    )
    d_up = (d_hidden * gate_pre * gate_sig).astype(jnp.bfloat16)
    d_act = jnp.stack([d_gate, d_up]).reshape(saved_act.shape)
    partial_sums = jnp.sum(hidden * d_piece, axis=1)
    own_partial = lax.psum_scatter(partial_sums, "etp", scatter_dimension=0, tiled=True)
    returned = lax.all_to_all(own_partial, "expert", split_axis=0, concat_axis=0, tiled=True)
    d_route = jnp.einsum(
        "ecj,ec->j",
        own_table,
        returned.reshape(expert_count, capacity),
        precision=lax.Precision.HIGHEST,
    ).reshape(tok_count, 2)
    summed = lax.psum(grad_part, "dp")
    half_width = width // lax.axis_size("dp")
    kept = lax.dynamic_slice_in_dim(summed, lax.axis_index("dp") * half_width, half_width, 1)
    d_weight = kept.astype(jnp.bfloat16)[None]
    return (d_act, d_weight, d_route)


def solution(mesh):
    placed = (
        P(("expert", "etp", "dp"), None),
        P(("expert", "etp", "dp"), None),
        P(("expert", "etp", "dp"), None),
        P(None, "dp", "expert", None, "etp"),
        P("expert", "etp", None),
    )
    return jax.shard_map(
        per_device,
        mesh=mesh,
        in_specs=placed,
        out_specs=(
            P(None, "dp", "expert", None, "etp"),
            P("expert", "etp", "dp"),
            P(("expert", "etp", "dp"), None),
        ),
        check_vma=False,
    )
```

profile of v0, /device:TPU:1, one launch (start us, length us, event | category | flops | bytes accessed | tf_op | source)
XLA Modules:
  0.0 449.0 jit_solution(150697266367591279)
XLA Ops:
  7.2 0.0 copy-start
  7.2 0.0 all-gather.2.cloned.1.call-start
  7.2 0.9 copy.25
  8.1 0.1 eq.69
  8.2 0.1 fusion.22
  8.3 0.2 select_reduce_fusion
  8.5 0.0 copy-start.1
  8.5 0.9 broadcast_in_dim.4
  9.4 0.2 convolution_convert_fusion
  9.6 0.2 copy.28
  9.8 24.0 %all_to_all.30 = bf16[8,4,3072]{2,1,0:T(4,128)(2,1)S(1)} all-to-all(bf16[8,4,3072]{2,1,0:T(4,128)(2,1)S(1)} %copy.28), channel_id=1, replica_groups=mesh['expert'=8,'etp'=32,'dp'=2] {'expert'}, dimensions={0} | all-to-all | bytes 393216 | tf_op jit(solution)/shard_map/all_to_all | solution.py:44
  33.7 0.7 all_to_all.24
  34.5 0.0 all-gather.2.cloned.1.call-update
  34.5 0.7 copy.26
  35.2 0.1 reshape.110
  35.3 0.1 fusion.18
  35.5 0.7 copy.27
  36.2 7.9 %all-to-all-start = ((bf16[8,4,1]{1,2,0:T(2,128)(2,1)}), bf16[8,4,1]{1,2,0:T(2,128)(2,1)S(1)}, u32[]{:S(2)}, u32[]{:S(2)}) async-start(bf16[8,4,1]{1,2,0:T(2,128)(2,1)} %copy.27), calls=%async_computation | async-start | bytes 8192 | tf_op jit(solution)/shard_map/all_to_all | solution.py:51
  44.1 0.1 eq.82
  44.1 1.3 fusion.28
  45.4 0.2 copy.39
  45.6 0.2 copy.40
  45.9 0.0 copy-done.1
  45.9 0.6 fusion.29
  47.0 0.1 iota_compare_fusion.1
  47.1 0.1 iota_compare_fusion
  47.2 0.1 broadcast_and_fusion
  47.9 5.3 %all-to-all-done = bf16[8,4,1]{1,2,0:T(2,128)(2,1)S(1)} async-done(((bf16[8,4,1]{1,2,0:T(2,128)(2,1)}), bf16[8,4,1]{1,2,0:T(2,128)(2,1)S(1)}, u32[]{:S(2)}, u32[]{:S(2)}) %all-to-all-start) | async-done | bytes 96 | tf_op jit(solution)/shard_map/all_to_all | solution.py:51
  53.2 0.1 reshape.105
  53.3 0.2 dynamic-update-slice
  53.6 181.8 %all-reduce = bf16[1024]{0:T(1024)(128)(2,1)S(1)} all-reduce(bf16[1024]{0:T(1024)(128)(2,1)S(1)} %dynamic-update-slice), channel_id=1, replica_groups=mesh['expert'=8,'etp'=32,'dp'=2] {'etp'}, use_global_device_ids=true, to_apply=%add | all-reduce | flops 1024 | bytes 4096
  235.4 15.5 %all-gather.2.cloned.1.call-done = bf16[1024,3072]{1,0:T(8,128)(2,1)} async-done(((bf16[32,3072]{1,0:T(8,128)(2,1)}), bf16[1024,3072]{1,0:T(8,128)(2,1)}) %all-gather.2.cloned.1.call-update) | async-done | bytes 6291472 | tf_op jit(solution)/shard_map/all_gather | solution.py:59
  250.8 0.0 copy-done
  250.8 6.1 %multiply_reduce_fusion = (f32[1024]{0:T(1024)S(1)}, bf16[1,1024,256]{1,2,0:T(8,128)(2,1)}, bf16[1,1024,256]{1,2,0:T(8,128)(2,1)}) fusion(bf16[1,1,1,1024,256]{3,4,2,1,0:T(8,128)(2,1)S(1)} %copy.39, bf16[1,1,1,1024,256]{3,4,2,1,0:T(8,128)(2,1)S(1)} %copy.40, f32[1024]{0:T(1024)S(1)} %convert_element_type.45, ...), kind=kOutput, calls=%fused_computation.20 | convolution fusion | flops 1615854592 | bytes 9969664 | tf_op jit(solution)/shard_map/dot_general | solution.py:66
  256.9 133.0 %all-reduce.1 = f32[1024]{0:T(1024)S(1)} all-reduce(f32[1024]{0:T(1024)S(1)} %get-tuple-element.12), channel_id=2, replica_groups=mesh['expert'=8,'etp'=32,'dp'=2] {'etp'}, use_global_device_ids=true, to_apply=%region_4.5.clone | all-reduce | flops 1024 | bytes 8192
  389.9 0.1 dynamic-slice.2
  390.0 0.7 all_to_all.25
  390.6 12.9 %all-to-all-start.2 = ((f32[8,4,1]{1,2,0:T(1,128)}), f32[8,4,1]{1,2,0:T(1,128)S(1)}, u32[]{:S(2)}, u32[]{:S(2)}) async-start(f32[8,4,1]{1,2,0:T(1,128)} %bitcast.12), calls=%async_computation.2 | async-start | bytes 8192 | tf_op jit(solution)/shard_map/all_to_all | solution.py:77
  403.6 6.4 %fusion.12 = f32[256,3072]{1,0:T(8,128)} fusion(bf16[1024,3072]{1,0:T(8,128)(2,1)} %all-gather.2.cloned.1.call-done, f32[1024]{0:T(1024)S(1)} %convert_element_type.45, bf16[1,1,1,1024,256]{3,4,2,1,0:T(8,128)(2,1)S(1)} %copy.39, bf16[1,1,1,1024,256]{3,4,2,1,0:T(8,128)(2,1)S(1)} %copy.40), kind=kOutput, calls=%fused_computation.23 | convolution fusion | flops 1612972032 | bytes 10489856 | tf_op jit(solution)/shard_map/dot_general | solution.py:63
  410.0 27.8 %all-reduce.3 = bf16[256,3072]{1,0:T(8,128)(2,1)S(1)} all-reduce(f32[256,3072]{1,0:T(8,128)} %fusion.12), channel_id=1, replica_groups=mesh['expert'=8,'etp'=32,'dp'=2] {'dp'}, use_global_device_ids=true, to_apply=%region_2.3 | all-reduce | flops 786432 | bytes 4718592 | tf_op jit(solution)/shard_map/psum | solution.py:84
  437.8 0.9 fusion.11
  438.7 1.3 maximum_bitcast_fusion
  440.0 1.3 copy.34
  441.3 0.0 all-to-all-done.2
  441.3 0.1 copy.33
  441.4 0.8 fusion.16
  (8 shorter events, 0.1 us)
Async XLA Ops:
  7.2 243.7 %copy-start = (bf16[1,256,3072]{2,1,0:T(8,128)(2,1)S(1)}, bf16[1,256,3072]{2,1,0:T(8,128)(2,1)}, u32[]{:S(2)}) copy-start(bf16[1,256,3072]{2,1,0:T(8,128)(2,1)} %param.9) | copy-start | bytes 4718596
  7.2 243.7 %all-gather.2.cloned.1.call-start = ((), (), s32[]{:S(2)}) async-start(), calls=%async_computation.3 | async-start | bytes 6488064 | tf_op jit(solution)/shard_map/all_gather | solution.py:59
  8.5 37.4 %copy-start.1 = (u32[512]{0:T(512)S(1)}, u32[512]{0:T(512)}, u32[]{:S(2)}) copy-start(u32[512]{0:T(512)} %constant.25) | copy-start | bytes 6148
  36.2 17.0 %all-to-all-start = ((bf16[8,4,1]{1,2,0:T(2,128)(2,1)}), bf16[8,4,1]{1,2,0:T(2,128)(2,1)S(1)}, u32[]{:S(2)}, u32[]{:S(2)}) async-start(bf16[8,4,1]{1,2,0:T(2,128)(2,1)} %copy.27), calls=%async_computation | async-start | bytes 8192 | tf_op jit(solution)/shard_map/all_to_all | solution.py:51
  390.6 50.7 %all-to-all-start.2 = ((f32[8,4,1]{1,2,0:T(1,128)}), f32[8,4,1]{1,2,0:T(1,128)S(1)}, u32[]{:S(2)}, u32[]{:S(2)}) async-start(f32[8,4,1]{1,2,0:T(1,128)} %bitcast.12), calls=%async_computation.2 | async-start | bytes 8192 | tf_op jit(solution)/shard_map/all_to_all | solution.py:77
Sparse Core Ops, SparseCore 0:
  34.6 216.1 all-gather.1
where the time goes:
time: 450 us; the launch traced here: 449 us
  blocking collectives  367 us (82%)
  starting transfers between devices  20.8 us (5%)
  waiting for transfers between devices  20.8 us (5%)
  between operations  15.4 us (3%)
  matrix products  13.6 us (3%)
  local copies, waits for them, and re-layouts  10 us (2%)
    unnamed x2, blocking collectives  315 us
    psum x1, blocking collectives, per_device(): summed = lax.psum(grad_part, 'dp')  27.8 us
    all_to_all x1, blocking collectives, per_device(): lax.all_to_all(outgoing.reshape(expert_count * capacity, width), 'expert'...  24 us
    all_gather x1, waiting for transfers between devices, per_device(): piece_rows = lax.all_gather(received, 'etp', axis=0, tiled=True)  15.5 us
    all_to_all x1, starting transfers between devices, per_device(): lax.all_to_all(own_partial, 'expert', split_axis=0, concat_axis=0, tiled=...  12.9 us
  transfers between devices with their start and end apart: 3, of which 2 were waited for; matrix products, arithmetic and copies ran while one was open for 3% of the time, Pallas kernels for 0%

commit v1 on v0

v1 whole, which is shorter than its diff:
```python
import jax
import jax.numpy as jnp
from jax import lax
from jax.experimental import pallas as pl
from jax.experimental.pallas import tpu as pltpu
from jax.sharding import PartitionSpec as P

MESH = pl.DeviceIdType.MESH
F32 = jnp.float32
BF16 = jnp.bfloat16
D = 3072
HALF = D // 2
FOLD = D // 4
ORDER = (0, 1, 3, 2)


def iota(shape, axis):
    return lax.broadcasted_iota(jnp.int32, shape, axis)


def kernel(
    tok_ref, route_ref, weight_ref, act_hbm, w_hbm,
    dact_hbm, dw_hbm, droute_ref,
    act, w, wt, outgoing, zbuf, rows, hid, cgate, cup, hidt, dact, grad, grad_in, dw,
    psum, psum_in, colsum, colsum_in,
    local_sem, zsend, zrecv, gsend, grecv, psend, precv, csend, crecv, xsend, xrecv,
):
    e = lax.axis_index("expert")
    t = lax.axis_index("etp")
    p = lax.axis_index("dp")
    x, y, zh = t // 8, (t // 2) % 4, t % 2
    z = zh * 8 + e
    quad = z // 4
    col = x * 4 + y

    def at(xx, yy, zz):
        return (zz % 8, xx * 8 + yy * 2 + zz // 8, p)

    def at_col(cc):
        return at(cc // 4, cc % 4, z)

    sibling = (e, t, 1 - p)
    xr, xl, yr, yl = (x + 1) % 4, (x + 3) % 4, (y + 1) % 4, (y + 3) % 4

    barrier = pltpu.get_barrier_semaphore()
    for k in range(1, 16):
        pl.semaphore_signal(barrier, inc=1, device_id=at(x, y, (z + k) % 16), device_id_type=MESH)
        pl.semaphore_signal(barrier, inc=1, device_id=at_col((col + k) % 16), device_id_type=MESH)
    pl.semaphore_signal(barrier, inc=1, device_id=sibling, device_id_type=MESH)

    load_act = pltpu.make_async_copy(act_hbm, act, local_sem.at[0])
    load_w = pltpu.make_async_copy(w_hbm, w, local_sem.at[1])
    load_act.start()
    load_w.start()

    spread = (iota((8, 128), 1) % 8 == iota((8, 128), 0)).astype(BF16)
    routes = jnp.dot(route_ref[...].astype(F32).astype(BF16), spread, preferred_element_type=F32)
    gates = jnp.dot(weight_ref[...], spread, preferred_element_type=F32)
    row, lane = iota((128, 128), 0), iota((128, 128), 1)
    row_e = (row // 16).astype(F32)
    first, second = routes[0:1] == row_e, routes[1:2] == row_e
    named = jnp.logical_or(first, second)
    earlier = jnp.logical_and(row // 8 == lane // 8, row < lane).astype(BF16)
    rank = jnp.dot(named.astype(F32).astype(BF16), earlier, preferred_element_type=F32)
    hit = jnp.logical_and(named, rank == (row % 4).astype(F32))
    hit = jnp.logical_and(hit, (row // 4) % 4 == lane // 8)
    pick = jnp.where(hit, jnp.where(first, gates[0:1], gates[1:2]), 0.0).astype(BF16)
    token = tok_ref[...].astype(F32)
    folded = jnp.concatenate([token[:, i * FOLD : (i + 1) * FOLD] for i in range(4)], axis=0)
    slots = jnp.dot(pick[:, 0:32], folded.astype(BF16), preferred_element_type=F32)
    outgoing[...] = slots.astype(BF16).reshape(8, 16, FOLD)

    pl.semaphore_wait(barrier, 31)

    sends = []
    for qrel in ORDER:
        for k in range(4):
            if qrel == 0 and k == 0:
                continue
            zz = ((quad + qrel) % 4) * 4 + (z + k) % 4
            copy = pltpu.make_async_remote_copy(
                src_ref=outgoing.at[zz % 8],
                dst_ref=zbuf.at[z],
                send_sem=zsend.at[len(sends)],
                recv_sem=zrecv.at[quad],
                device_id=at(x, y, zz),
                device_id_type=MESH,
            )
            copy.start()
            sends.append(copy)
    zbuf[z] = outgoing[e]

    mrow, mcol = iota((64, 64), 0), iota((64, 64), 1)
    unfold = jnp.logical_and(mrow // 16 == (mcol // 4) % 4, (mrow // 4) % 4 == mcol // 16)
    unfold = jnp.logical_and(unfold, mrow % 4 == mcol % 4).astype(F32).astype(BF16)

    def assemble(j):
        q = (quad + ORDER[j]) % 4
        count = 3 if j == 0 else 4
        landed = zbuf.at[pl.ds(0, count)]
        pltpu.make_async_copy(landed, landed, zrecv.at[q]).wait()
        block = zbuf[pl.ds(q * 4, 4)].reshape(64, FOLD)
        flat = jnp.dot(unfold, block, preferred_element_type=F32).astype(BF16)
        for i in range(4):
            rows[j, x, y, :, i * FOLD : (i + 1) * FOLD] = flat[i * 16 : (i + 1) * 16]

    every = pl.ds(0, 4)
    whole = (pl.ds(0, HALF), pl.ds(HALF, HALF))
    part = (
        (pl.ds(0, FOLD), pl.ds(FOLD, FOLD)),
        (pl.ds(HALF, FOLD), pl.ds(HALF + FOLD, FOLD)),
    )

    def push(j, slot, ref, target):
        copy = pltpu.make_async_remote_copy(
            src_ref=ref,
            dst_ref=ref,
            send_sem=gsend.at[j, slot],
            recv_sem=grecv.at[j, slot],
            device_id=target,
            device_id_type=MESH,
        )
        copy.start()
        sends.append(copy)
        return copy

    right, left = (at(xr, y, z), at(x, yr, z)), (at(xl, y, z), at(x, yl, z))

    def line(j, half, xx, yy, columns):
        return rows.at[j, xx, yy, :, columns]

    def one(j):
        own = [line(j, h, x, y, whole[h]) for h in range(2)]
        return [push(j, 8 * h + d, own[h], (right, left)[d][h]) for d in range(2) for h in range(2)]

    def one_forward(j, got):
        copies = []
        for d in range(2):
            for h in range(2):
                got[2 * d + h].wait_recv()
                side = ((xl, yl), (xr, yr))[d]
                xx, yy = (side[0], y) if h == 0 else (x, side[1])
                ref = line(j, h, xx, yy, part[h][d])
                copies.append(push(j, 8 * h + 2 + d, ref, (right, left)[d][h]))
        return copies

    def two(j, got):
        for copy in got:
            copy.wait_recv()
        copies = []
        for d in range(2):
            for h in range(2):
                xx, yy = (every, y) if h == 0 else (x, every)
                ref = line(j, h, xx, yy, whole[h])
                copies.append(push(j, 8 * h + 4 + d, ref, (right, left)[d][1 - h]))
        return copies

    def two_forward(j, got):
        copies = []
        for d in range(2):
            for h in range(2):
                got[2 * d + h].wait_recv()
                side = ((xl, yl), (xr, yr))[d]
                xx, yy = (every, side[1]) if h == 0 else (side[0], every)
                ref = line(j, h, xx, yy, part[h][d])
                copies.append(push(j, 8 * h + 6 + d, ref, (right, left)[d][1 - h]))
        return copies

    def prepare(j):
        q = (quad + ORDER[j]) % 4

        @pl.loop(0, 16)
        def _(c):
            g = act[0, c, q].astype(F32)
            u = act[1, c, q].astype(F32)
            sig = 1.0 / (1.0 + jnp.exp(-g))
            gs = g * sig
            h = gs * u
            at_rows = pl.ds(pl.multiple_of(c * 16, 16), 16)
            hid[j, at_rows, :] = h
            cup[j, at_rows, :] = gs
            cgate[j, at_rows, :] = u * sig * (1.0 + g * (1.0 - sig))

        hidt[j] = hid[j].T.astype(BF16)

    def transpose_w():
        @pl.loop(0, D // 256)
        def _(k):
            at_cols = pl.ds(pl.multiple_of(k * 256, 256), 256)
            wt[at_cols, :] = w[:, at_cols].astype(F32).T.astype(BF16)

    stores = []

    def first_product(j):
        q = (quad + ORDER[j]) % 4
        d_out = jnp.dot(rows[j].reshape(256, D), wt[...], preferred_element_type=F32)
        dact[0, :, q] = (d_out * cgate[j]).astype(BF16).reshape(16, 16, 256)
        dact[1, :, q] = (d_out * cup[j]).astype(BF16).reshape(16, 16, 256)
        prod = d_out * hid[j]
        total = jnp.sum((prod[:, 0:128] + prod[:, 128:256]).T, axis=0, keepdims=True)
        psum[0, j : j + 1, :] = total[:, 0:128]
        psum[1, j : j + 1, :] = total[:, 128:256]
        store = pltpu.make_async_copy(
            dact.at[:, :, q], dact_hbm.at[:, :, q], local_sem.at[2 + j]
        )
        store.start()
        stores.append(store)

    def second_product(j, half):
        for k in range(3):
            out_cols = slice(k * 512, (k + 1) * 512)
            in_cols = pl.ds(pl.multiple_of(half * HALF + k * 512, 512), 512)
            block = rows[j, :, :, :, in_cols].reshape(256, 512)
            term = jnp.dot(hidt[j], block, preferred_element_type=F32)
            if j == 0:
                grad[half, :, out_cols] = term
            else:
                grad[half, :, out_cols] += term

    def compute(j):
        first_product(j)
        second_product(j, 0)
        second_product(j, 1)

    def landed(copies):
        for copy in copies:
            copy.wait_recv()

    assemble(0)
    a0 = one(0)
    load_act.wait()
    prepare(0)
    b0 = one_forward(0, a0)
    assemble(1)
    a1 = one(1)
    c0 = two(0, b0)
    b1 = one_forward(1, a1)
    load_w.wait()
    transpose_w()
    assemble(2)
    a2 = one(2)
    c1 = two(1, b1)
    prepare(1)
    d0 = two_forward(0, c0)
    b2 = one_forward(2, a2)
    assemble(3)
    a3 = one(3)
    c2 = two(2, b2)
    prepare(2)
    d1 = two_forward(1, c1)
    b3 = one_forward(3, a3)
    prepare(3)
    landed(d0)
    compute(0)
    c3 = two(3, b3)
    d2 = two_forward(2, c2)
    landed(d1)
    compute(1)
    d3 = two_forward(3, c3)
    landed(d2)
    compute(2)
    landed(d3)
    first_product(3)

    for k in range(1, 16):
        cc = (col + k) % 16
        copy = pltpu.make_async_remote_copy(
            src_ref=psum.at[cc // 8],
            dst_ref=psum_in.at[col],
            send_sem=psend.at[k - 1],
            recv_sem=precv,
            device_id=at_col(cc),
            device_id_type=MESH,
        )
        copy.start()
        sends.append(copy)
    psum_in[col] = psum[col // 8]

    second_product(3, 1 - p)
    swap = pltpu.make_async_remote_copy(
        src_ref=grad.at[1 - p],
        dst_ref=grad_in,
        send_sem=xsend,
        recv_sem=xrecv,
        device_id=sibling,
        device_id_type=MESH,
    )
    swap.start()
    second_product(3, p)

    arrived = psum_in.at[pl.ds(0, 15)]
    pltpu.make_async_copy(arrived, arrived, precv).wait()
    total = jnp.sum(psum_in[...], axis=0)
    for j in range(4):
        colsum[j] = total[j : j + 1]
    for k in range(1, 16):
        zz = (z + k) % 16
        rel = (zz // 4 - quad + 4) % 4
        j = jnp.where(rel == 3, 2, jnp.where(rel == 2, 3, rel))
        copy = pltpu.make_async_remote_copy(
            src_ref=colsum.at[j],
            dst_ref=colsum_in.at[z],
            send_sem=csend.at[k - 1],
            recv_sem=crecv,
            device_id=at(x, y, zz),
            device_id_type=MESH,
        )
        copy.start()
        sends.append(copy)
    colsum_in[z] = colsum[0]

    swap.wait_recv()
    for k in range(3):
        cols = slice(k * 512, (k + 1) * 512)
        dw[:, cols] = (grad[p, :, cols] + grad_in[:, cols]).astype(BF16)
    store_w = pltpu.make_async_copy(dw, dw_hbm, local_sem.at[6])
    store_w.start()

    arrived = colsum_in.at[pl.ds(0, 15)]
    pltpu.make_async_copy(arrived, arrived, crecv).wait()
    value = jnp.zeros((128, 128), F32)
    for i in range(8):
        both = colsum_in[i] + colsum_in[i + 8]
        value = jnp.where(row // 16 == i, both, value)
    mine = (col % 8) * 16 + (z % 4) * 4
    value = jnp.sum(jnp.where(lane == mine + row % 4, value, 0.0), axis=1, keepdims=True)
    for k, match in enumerate((first, second)):
        chosen = jnp.where(jnp.logical_and(hit, match), value, 0.0)
        score = jnp.sum(chosen, axis=0, keepdims=True) / gates[k : k + 1]
        droute_ref[k : k + 1, :] = score[:, 0:8]

    swap.wait_send()
    for copy in sends:
        copy.wait_send()
    for store in stores:
        store.wait()
    store_w.wait()


def per_device(out_grad, routes, route_weight, saved_act, w_down):
    vmem, hbm = pl.BlockSpec(memory_space=pltpu.VMEM), pl.BlockSpec(memory_space=pl.ANY)
    dma = pltpu.SemaphoreType.DMA
    d_act, d_weight, d_route = pl.pallas_call(
        kernel,
        out_shape=(
            jax.ShapeDtypeStruct((2, 16, 4, 16, 256), BF16),
            jax.ShapeDtypeStruct((256, HALF), BF16),
            jax.ShapeDtypeStruct((2, 8), F32),
        ),
        in_specs=[vmem, vmem, vmem, hbm, hbm],
        out_specs=(hbm, hbm, vmem),
        scratch_shapes=[
            pltpu.VMEM((2, 16, 4, 16, 256), BF16),
            pltpu.VMEM((256, D), BF16),
            pltpu.VMEM((D, 256), BF16),
            pltpu.VMEM((8, 16, FOLD), BF16),
            pltpu.VMEM((16, 16, FOLD), BF16),
            pltpu.VMEM((4, 4, 4, 16, D), BF16),
            pltpu.VMEM((4, 256, 256), F32),
            pltpu.VMEM((4, 256, 256), F32),
            pltpu.VMEM((4, 256, 256), F32),
            pltpu.VMEM((4, 256, 256), BF16),
            pltpu.VMEM((2, 16, 4, 16, 256), BF16),
            pltpu.VMEM((2, 256, HALF), F32),
            pltpu.VMEM((256, HALF), F32),
            pltpu.VMEM((256, HALF), BF16),
            pltpu.VMEM((2, 4, 128), F32),
            pltpu.VMEM((16, 4, 128), F32),
            pltpu.VMEM((4, 1, 128), F32),
            pltpu.VMEM((16, 1, 128), F32),
            dma((7,)),
            dma((15,)),
            dma((4,)),
            dma((4, 16)),
            dma((4, 16)),
            dma((15,)),
            dma,
            dma((15,)),
            dma,
            dma,
            dma,
        ],
        compiler_params=pltpu.CompilerParams(
            collective_id=0, has_side_effects=True, vmem_limit_bytes=48 * 1024 * 1024
        ),
    )(
        out_grad,
        routes.T,
        route_weight.T,
        saved_act.reshape(2, 16, 4, 16, 256),
        w_down[0],
    )
    return (
        d_act.reshape(saved_act.shape),
        d_weight[None],
        d_route.T,
    )


def solution(mesh):
    placed = (
        P(("expert", "etp", "dp"), None),
        P(("expert", "etp", "dp"), None),
        P(("expert", "etp", "dp"), None),
        P(None, "dp", "expert", None, "etp"),
        P("expert", "etp", None),
    )
    return jax.shard_map(
        per_device,
        mesh=mesh,
        in_specs=placed,
        out_specs=(
            P(None, "dp", "expert", None, "etp"),
            P("expert", "etp", "dp"),
            P(("expert", "etp", "dp"), None),
        ),
        check_vma=False,
    )
```

time: 450 us -> 94.3 us (0.21)
  the two profiles are of different devices: /device:TPU:1 before, /device:TPU:32 now
where the time goes in v1:
time: 94.3 us; the launch traced here: 94.1 us
  Pallas kernels  86.2 us (91%)
  local copies, waits for them, and re-layouts  7.17 us (8%)
    pallas_call x1, Pallas kernels, per_device(): pl.pallas_call(kernel, out_shape=(jax.ShapeDtypeStruct((2, 16, 4, 16, 256...  86.2 us
    unnamed x13, local copies, waits for them, and re-layouts  7.17 us

profile of v1, /device:TPU:32, one launch (start us, length us, event | category | flops | bytes accessed | tf_op | source)
XLA Modules:
  0.0 94.1 jit_solution(9503109662016016994)
XLA Ops:
  0.6 0.0 copy-start
  0.6 1.4 %copy-done = bf16[1,256,3072]{2,1,0:T(8,128)(2,1)S(1)} copy-done((bf16[1,256,3072]{2,1,0:T(8,128)(2,1)S(1)}, bf16[1,256,3072]{2,1,0:T(8,128)(2,1)}, u32[]{:S(2)}) %copy-start) | copy-done | bytes 1572888
  2.0 0.0 copy-start.1
  2.0 1.2 %copy-done.1 = bf16[2,1,1,1024,256]{4,3,2,1,0:T(8,128)(2,1)S(1)} copy-done((bf16[2,1,1,1024,256]{4,3,2,1,0:T(8,128)(2,1)S(1)}, bf16[2,1,1,1024,256]{4,3,2,1,0:T(8,128)(2,1)}, u32[]{:S(2)}) %copy-start.1) | copy-done | bytes 1048600
  3.3 0.0 copy-start.2
  3.3 0.8 copy-done.2
  4.1 0.0 copy-start.3
  4.1 0.7 copy-done.3
  4.7 0.0 copy-start.4
  4.7 0.7 copy-done.4
  5.4 86.2 %shard_map.76 = (bf16[2,16,4,16,256]{4,3,2,1,0:T(8,128)(2,1)S(1)}, bf16[256,1536]{1,0:T(8,128)(2,1)S(1)}, f32[2,8]{1,0:T(2,128)S(1)}) custom-call(bf16[8,3072]{1,0:T(8,128)(2,1)S(1)} %copy-done.2, s32[2,8]{1,0:T(2,128)S(1)} %bitcast.13, bf16[2,8]{1,0:T(2,128)(2,1)S(1)} %bitcast.15, bf16[2,16,4,16,256]{4,3,2,1,0:T(8,128)(2,1)S(1)} %bitcast.10, ...), custom_call_target="tpu_custom_call" | custom-call | tf_op jit(solution)/shard_map/pallas_call | solution.py:343
  91.6 1.0 %copy.12 = bf16[2,1,1,1024,256]{4,3,2,1,0:T(8,128)(2,1)} copy(bf16[2,1,1,1024,256]{4,3,2,1,0:T(8,128)(2,1)S(1)} %bitcast.11) | data formatting | bytes 2097152
  92.6 0.9 copy.13
  93.5 0.6 copy.14
Async XLA Ops:
  0.6 1.4 %copy-start = (bf16[1,256,3072]{2,1,0:T(8,128)(2,1)S(1)}, bf16[1,256,3072]{2,1,0:T(8,128)(2,1)}, u32[]{:S(2)}) copy-start(bf16[1,256,3072]{2,1,0:T(8,128)(2,1)} %param.9) | copy-start | bytes 4718596
  2.0 1.2 %copy-start.1 = (bf16[2,1,1,1024,256]{4,3,2,1,0:T(8,128)(2,1)S(1)}, bf16[2,1,1,1024,256]{4,3,2,1,0:T(8,128)(2,1)}, u32[]{:S(2)}) copy-start(bf16[2,1,1,1024,256]{4,3,2,1,0:T(8,128)(2,1)} %param.8) | copy-start | bytes 3145732
  3.3 0.8 copy-start.2
  4.1 0.7 copy-start.3
  4.7 0.7 copy-start.4

commit v2 on v1

v2 whole, which is shorter than its diff:
```python
import jax
import jax.numpy as jnp
from jax import lax
from jax.experimental import pallas as pl
from jax.experimental.pallas import tpu as pltpu
from jax.sharding import PartitionSpec as P

MESH = pl.DeviceIdType.MESH
F32 = jnp.float32
BF16 = jnp.bfloat16
D = 3072
HALF = D // 2
FOLD = D // 4
NEAR = ((0, 1, 15, 2), (14, 13, 3, 4), (12, 11, 5, 6), (10, 9, 7, 8))


def iota(shape, axis):
    return lax.broadcasted_iota(jnp.int32, shape, axis)


def kernel(
    tok_hbm, route_hbm, weight_hbm, act_hbm, w_hbm,
    dact, dw, droute,
    tok_ref, route_ref, weight_ref, act, w, wt, outgoing, zbuf, rows, hid, cgate, cup, hidt, drel, grad, grad_in,
    last, last_in, psum, psum_in, colsum, colsum_in,
    local_sem, zsend, zrecv, gsend, grecv, psend, precv, csend, crecv, xsend, xrecv,
):
    e = lax.axis_index("expert")
    t = lax.axis_index("etp")
    p = lax.axis_index("dp")
    x, y, zh = t // 8, (t // 2) % 4, t % 2
    z = zh * 8 + e
    col = x * 4 + y

    def at(xx, yy, zz):
        return (zz % 8, xx * 8 + yy * 2 + zz // 8, p)

    def at_col(cc):
        return at(cc // 4, cc % 4, z)

    sibling = (e, t, 1 - p)
    xr, xl, yr, yl = (x + 1) % 4, (x + 3) % 4, (y + 1) % 4, (y + 3) % 4

    loads = []
    for k, (src, dst) in enumerate(
        ((route_hbm, route_ref), (weight_hbm, weight_ref), (tok_hbm, tok_ref), (act_hbm, act), (w_hbm, w))
    ):
        loads.append(pltpu.make_async_copy(src, dst, local_sem.at[k]))
        loads[k].start()
    load_act, load_w = loads[3:]

    barrier = pltpu.get_barrier_semaphore()
    for k in range(1, 16):
        pl.semaphore_signal(barrier, inc=1, device_id=at(x, y, (z + k) % 16), device_id_type=MESH)
        pl.semaphore_signal(barrier, inc=1, device_id=at_col((col + k) % 16), device_id_type=MESH)
    pl.semaphore_signal(barrier, inc=1, device_id=sibling, device_id_type=MESH)

    spread = (iota((8, 128), 1) % 8 == iota((8, 128), 0)).astype(BF16)
    for k in range(3):
        loads[k].wait()
    routes = jnp.dot(route_ref[...].astype(F32).astype(BF16), spread, preferred_element_type=F32)
    gates = jnp.dot(weight_ref[...], spread, preferred_element_type=F32)
    row, lane = iota((128, 128), 0), iota((128, 128), 1)
    row_e = (row // 16).astype(F32)
    first, second = routes[0:1] == row_e, routes[1:2] == row_e
    named = jnp.logical_or(first, second)
    earlier = jnp.logical_and(row // 8 == lane // 8, row < lane).astype(BF16)
    rank = jnp.dot(named.astype(F32).astype(BF16), earlier, preferred_element_type=F32)
    hit = jnp.logical_and(named, rank == (row % 4).astype(F32))
    hit = jnp.logical_and(hit, (row // 4) % 4 == lane // 8)
    pick = jnp.where(hit, jnp.where(first, gates[0:1], gates[1:2]), 0.0).astype(BF16)
    token = tok_ref[...].astype(F32)
    folded = jnp.concatenate([token[:, i * FOLD : (i + 1) * FOLD] for i in range(4)], axis=0)
    slots = jnp.dot(pick[:, 0:32], folded.astype(BF16), preferred_element_type=F32)
    outgoing[...] = slots.astype(BF16).reshape(8, 16, FOLD)

    pl.semaphore_wait(barrier, 31)

    sends = []

    def along(j):
        for k, near in enumerate(NEAR[j]):
            if near == 0:
                continue
            zz = (z + 16 - near) % 16
            copy = pltpu.make_async_remote_copy(
                src_ref=outgoing.at[zz % 8],
                dst_ref=zbuf.at[j, k],
                send_sem=zsend.at[j, k],
                recv_sem=zrecv.at[j],
                device_id=at(x, y, zz),
                device_id_type=MESH,
            )
            copy.start()
            sends.append(copy)

    along(0)
    along(1)
    zbuf[0, 0] = outgoing[e]

    mrow, mcol = iota((64, 64), 0), iota((64, 64), 1)
    unfold = jnp.logical_and(mrow // 16 == (mcol // 4) % 4, (mrow // 4) % 4 == mcol // 16)
    unfold = jnp.logical_and(unfold, mrow % 4 == mcol % 4).astype(F32).astype(BF16)

    def assemble(j):
        landed = zbuf.at[j, pl.ds(1, 3)] if j == 0 else zbuf.at[j]
        pltpu.make_async_copy(landed, landed, zrecv.at[j]).wait()
        block = zbuf[j].reshape(64, FOLD)
        flat = jnp.dot(unfold, block, preferred_element_type=F32).astype(BF16)
        for i in range(4):
            rows[j, x, y, :, i * FOLD : (i + 1) * FOLD] = flat[i * 16 : (i + 1) * 16]

    every = pl.ds(0, 4)
    whole = (pl.ds(0, HALF), pl.ds(HALF, HALF))
    part = (
        (pl.ds(0, FOLD), pl.ds(FOLD, FOLD)),
        (pl.ds(HALF, FOLD), pl.ds(HALF + FOLD, FOLD)),
    )

    def push(j, slot, ref, target):
        copy = pltpu.make_async_remote_copy(
            src_ref=ref,
            dst_ref=ref,
            send_sem=gsend.at[j, slot],
            recv_sem=grecv.at[j, slot],
            device_id=target,
            device_id_type=MESH,
        )
        copy.start()
        sends.append(copy)
        return copy

    right, left = (at(xr, y, z), at(x, yr, z)), (at(xl, y, z), at(x, yl, z))
    across = (at((x + 2) % 4, y, z), at(x, (y + 2) % 4, z))

    def line(j, half, xx, yy, columns):
        return rows.at[j, xx, yy, :, columns]

    def one(j):
        copies = []
        for d, target in enumerate((across, right, left)):
            for h in range(2):
                copies.append(push(j, 9 * h + d, line(j, h, x, y, whole[h]), target[h]))
        return copies

    def two(j, got):
        for copy in got:
            copy.wait_recv()
        copies = []
        for i in range(2):
            for d in range(2):
                for h in range(2):
                    xx, yy = (every, y) if h == 0 else (x, every)
                    ref = line(j, h, xx, yy, part[h][d if i == 0 else 1 - d])
                    copies.append(push(j, 9 * h + 3 + 2 * i + d, ref, (right, left)[d][1 - h]))
        return copies

    def onward(j, got):
        copies = []
        for d in range(2):
            for h in range(2):
                got[2 * d + h].wait_recv()
                side = ((xl, yl), (xr, yr))[d]
                xx, yy = (every, side[1]) if h == 0 else (side[0], every)
                ref = line(j, h, xx, yy, part[h][d])
                copies.append(push(j, 9 * h + 7 + d, ref, (right, left)[d][1 - h]))
        return copies + got[4:]

    frow, fcol = iota((64, 64), 0), iota((64, 64), 1)

    def chunked(place):
        near = jnp.zeros((64, 64), jnp.int32)
        for k, value in enumerate(sum(NEAR, ())):
            near = jnp.where(place // 4 == k, value, near)
        return 4 * ((z + near) % 16) + place % 4

    gather = (fcol == chunked(frow)).astype(F32).astype(BF16)
    scatter = (frow == chunked(fcol)).astype(F32).astype(BF16)

    def prepare(part):
        @pl.loop(part * 4, part * 4 + 4)
        def _(c):
            g = jnp.dot(gather, act[0, c], preferred_element_type=F32)
            u = jnp.dot(gather, act[1, c], preferred_element_type=F32)
            sig = 1.0 / (1.0 + jnp.exp(-g))
            gs = g * sig
            h = gs * u
            slope = u * sig * (1.0 + g * (1.0 - sig))
            at_rows = pl.ds(pl.multiple_of(c * 16, 16), 16)
            for j in range(4):
                mine = slice(j * 16, (j + 1) * 16)
                hid[j, at_rows, :] = h[mine]
                cup[j, at_rows, :] = gs[mine]
                cgate[j, at_rows, :] = slope[mine]

    def flip():
        for j in range(4):
            hidt[j] = hid[j].T.astype(BF16)

    def transpose_w():
        @pl.loop(0, D // 256)
        def _(k):
            at_cols = pl.ds(pl.multiple_of(k * 256, 256), 256)
            wt[at_cols, :] = w[:, at_cols].astype(F32).T.astype(BF16)

    def first_product(j):
        d_out = jnp.dot(rows[j].reshape(256, D), wt[...], preferred_element_type=F32)
        prod = d_out * hid[j]
        total = jnp.sum((prod[:, 0:128] + prod[:, 128:256]).T, axis=0, keepdims=True)
        psum[0, j, :, :] = total[:, 0:128]
        psum[1, j, :, :] = total[:, 128:256]
        return d_out

    def slopes(j, d_out):
        drel[0, :, j] = (d_out * cgate[j]).astype(BF16).reshape(16, 16, 256)
        drel[1, :, j] = (d_out * cup[j]).astype(BF16).reshape(16, 16, 256)

    def second_product(j, half, store):
        for k in range(3):
            in_cols = pl.ds(pl.multiple_of(half * HALF + k * 512, 512), 512)
            block = rows[j, :, :, :, in_cols].reshape(256, 512)
            store(slice(k * 512, (k + 1) * 512), jnp.dot(hidt[j], block, preferred_element_type=F32))

    def compute(j):
        slopes(j, first_product(j))
        for half in range(2):

            def store(cols, term):
                grad[half, :, cols] = term if j == 0 else grad[half, :, cols] + term

            second_product(j, half, store)

    def to_columns(js):
        for k in range(1, 16):
            cc = (col + k) % 16
            copy = pltpu.make_async_remote_copy(
                src_ref=psum.at[cc // 8, js],
                dst_ref=psum_in.at[col, js],
                send_sem=psend.at[js.start // 3, k - 1],
                recv_sem=precv.at[js.start // 3],
                device_id=at_col(cc),
                device_id_type=MESH,
            )
            copy.start()
            sends.append(copy)
        psum_in[col, js] = psum[col // 8, js]

    def along_column(js):
        arrived = psum_in.at[pl.ds(0, 15), js]
        pltpu.make_async_copy(arrived, arrived, precv.at[js.start // 3]).wait()
        for j in range(js.start, js.start + js.size):
            total = jnp.sum(psum_in[:, j], axis=0)
            for k, near in enumerate(NEAR[j]):
                turned = total if k == 0 else jnp.concatenate([total[:, 4 * k :], total[:, : 4 * k]], axis=1)
                colsum[j, k] = turned
                if near == 0:
                    colsum_in[z] = turned
                    continue
                copy = pltpu.make_async_remote_copy(
                    src_ref=colsum.at[j, k],
                    dst_ref=colsum_in.at[z],
                    send_sem=csend.at[j, k],
                    recv_sem=crecv,
                    device_id=at(x, y, (z + near) % 16),
                    device_id_type=MESH,
                )
                copy.start()
                sends.append(copy)

    def landed(copies):
        for copy in copies:
            copy.wait_recv()

    assemble(0)
    a0 = one(0)
    along(2)
    along(3)
    load_act.wait()
    prepare(0)
    prepare(1)
    b0 = two(0, a0)
    assemble(1)
    a1 = one(1)
    prepare(2)
    c0 = onward(0, b0)
    prepare(3)
    b1 = two(1, a1)
    load_w.wait()
    transpose_w()
    flip()
    assemble(2)
    a2 = one(2)
    c1 = onward(1, b1)
    landed(c0)
    compute(0)
    b2 = two(2, a2)
    assemble(3)
    a3 = one(3)
    c2 = onward(2, b2)
    landed(c1)
    compute(1)
    b3 = two(3, a3)
    landed(c2)
    compute(2)
    c3 = onward(3, b3)

    def to_sibling(i, src, dst):
        copy = pltpu.make_async_remote_copy(
            src_ref=src, dst_ref=dst, send_sem=xsend.at[i], recv_sem=xrecv.at[i], device_id=sibling, device_id_type=MESH
        )
        copy.start()
        sends.append(copy)
        return copy

    for copy in sends[:-22]:
        copy.wait_send()
    sends = sends[-22:]
    most = to_sibling(0, grad.at[1 - p], grad_in)
    to_columns(pl.ds(0, 3))
    landed(c3)
    d_out = first_product(3)
    to_columns(pl.ds(3, 1))

    def store_last(cols, term):
        last[:, cols] = term.astype(BF16)

    def store_grad(cols, term):
        grad[p, :, cols] += term

    second_product(3, 1 - p, store_last)
    rest = to_sibling(1, last, last_in)
    along_column(pl.ds(0, 3))
    slopes(3, d_out)
    along_column(pl.ds(3, 1))
    second_product(3, p, store_grad)
    for i in range(2):
        for c in range(16):
            dact[i, c] = jnp.dot(scatter, drel[i, c].reshape(64, 256), preferred_element_type=F32).astype(BF16)

    most.wait_recv()
    rest.wait_recv()
    for k in range(3):
        cols = slice(k * 512, (k + 1) * 512)
        dw[:, cols] = (grad[p, :, cols] + grad_in[:, cols] + last_in[:, cols].astype(F32)).astype(BF16)
    arrived = colsum_in.at[pl.ds(0, 15)]
    pltpu.make_async_copy(arrived, arrived, crecv).wait()
    value = jnp.zeros((128, 128), F32)
    for i in range(8):
        both = colsum_in[i] + colsum_in[i + 8]
        value = jnp.where(row // 16 == i, both, value)
    mine = (col % 8) * 16
    value = jnp.sum(jnp.where(lane == mine + row % 4, value, 0.0), axis=1, keepdims=True)
    for k, match in enumerate((first, second)):
        chosen = jnp.where(jnp.logical_and(hit, match), value, 0.0)
        score = jnp.sum(chosen, axis=0, keepdims=True) / gates[k : k + 1]
        droute[k : k + 1, :] = score[:, 0:8]
    for copy in sends:
        copy.wait_send()


def finish(dact_in, dw_in, droute_in, dact, dw, droute, sem):
    copies = [pltpu.make_async_copy(dw_in, dw, sem.at[0]), pltpu.make_async_copy(droute_in, droute, sem.at[1])]
    for i in range(4):
        quarter = pl.ds(4 * i, 4)
        copies.append(pltpu.make_async_copy(dact_in.at[:, quarter], dact.at[:, quarter], sem.at[2 + i]))
    for copy in copies:
        copy.start()
    for copy in copies:
        copy.wait()


def per_device(out_grad, routes, route_weight, saved_act, w_down):
    hbm, anywhere = pl.BlockSpec(memory_space=pltpu.HBM), pl.BlockSpec(memory_space=pl.ANY)
    shapes = (
        jax.ShapeDtypeStruct((2, 16, 64, 256), BF16),
        jax.ShapeDtypeStruct((256, HALF), BF16),
        jax.ShapeDtypeStruct((2, 8), F32),
    )
    dma = pltpu.SemaphoreType.DMA
    results = pl.pallas_call(
        kernel,
        out_shape=shapes,
        in_specs=[hbm] * 5,
        out_specs=(pl.BlockSpec(memory_space=pltpu.VMEM),) * 3,
        scratch_shapes=[
            pltpu.VMEM((8, D), BF16),
            pltpu.VMEM((2, 8), jnp.int32),
            pltpu.VMEM((2, 8), BF16),
            pltpu.VMEM((2, 16, 64, 256), BF16),
            pltpu.VMEM((256, D), BF16),
            pltpu.VMEM((D, 256), BF16),
            pltpu.VMEM((8, 16, FOLD), BF16),
            pltpu.VMEM((4, 4, 16, FOLD), BF16),
            pltpu.VMEM((4, 4, 4, 16, D), BF16),
            pltpu.VMEM((4, 256, 256), F32),
            pltpu.VMEM((4, 256, 256), F32),
            pltpu.VMEM((4, 256, 256), F32),
            pltpu.VMEM((4, 256, 256), BF16),
            pltpu.VMEM((2, 16, 4, 16, 256), BF16),
            pltpu.VMEM((2, 256, HALF), F32),
            pltpu.VMEM((256, HALF), F32),
            pltpu.VMEM((256, HALF), BF16),
            pltpu.VMEM((256, HALF), BF16),
            pltpu.VMEM((2, 4, 1, 128), F32),
            pltpu.VMEM((16, 4, 1, 128), F32),
            pltpu.VMEM((4, 4, 1, 128), F32),
            pltpu.VMEM((16, 1, 128), F32),
            dma((5,)),
            dma((4, 4)),
            dma((4,)),
            dma((4, 18)),
            dma((4, 18)),
            dma((2, 15)),
            dma((2,)),
            dma((4, 4)),
            dma,
            dma((2,)),
            dma((2,)),
        ],
        compiler_params=pltpu.CompilerParams(
            collective_id=0, has_side_effects=True, vmem_limit_bytes=40 * 1024 * 1024
        ),
    )(
        *(
            pltpu.with_memory_space_constraint(value, pltpu.HBM)
            for value in (out_grad, routes.T, route_weight.T, saved_act.reshape(2, 16, 64, 256), w_down[0])
        )
    )
    d_act, d_weight, d_route = pl.pallas_call(
        finish,
        out_shape=shapes,
        in_specs=[anywhere] * 3,
        out_specs=(hbm,) * 3,
        scratch_shapes=[dma((6,))],
        compiler_params=pltpu.CompilerParams(vmem_limit_bytes=2 * 1024 * 1024),
    )(*results)
    return (
        d_act.reshape(saved_act.shape),
        d_weight[None],
        d_route.T,
    )


def solution(mesh):
    placed = (
        P(("expert", "etp", "dp"), None),
        P(("expert", "etp", "dp"), None),
        P(("expert", "etp", "dp"), None),
        P(None, "dp", "expert", None, "etp"),
        P("expert", "etp", None),
    )
    return jax.shard_map(
        per_device,
        mesh=mesh,
        in_specs=placed,
        out_specs=(
            P(None, "dp", "expert", None, "etp"),
            P("expert", "etp", "dp"),
            P(("expert", "etp", "dp"), None),
        ),
        check_vma=False,
    )
```

time: 94.3 us -> 75.7 us (0.80)
  the two profiles are of different devices: /device:TPU:32 before, /device:TPU:2 now
where the time goes in v2:
time: 75.7 us; the launch traced here: 75.6 us
  Pallas kernels  75 us (99%)
    pallas_call x1, Pallas kernels, per_device(): pl.pallas_call(kernel, out_shape=shapes, in_specs=[hbm] * 5, out_specs=(p...  73.7 us

profile of v2, /device:TPU:2, one launch (start us, length us, event | category | flops | bytes accessed | tf_op | source)
XLA Modules:
  0.0 75.6 jit_solution(1008159505361354733)
XLA Ops:
  0.6 73.7 %shard_map.76 = (bf16[2,16,64,256]{3,2,1,0:T(8,128)(2,1)S(1)}, bf16[256,1536]{1,0:T(8,128)(2,1)S(1)}, f32[2,8]{1,0:T(2,128)S(1)}) custom-call(bf16[8,3072]{1,0:T(8,128)(2,1)} %tok_hbm.1, s32[2,8]{1,0:T(2,128)} %bitcast.11, bf16[2,8]{1,0:T(2,128)(2,1)} %bitcast.12, bf16[2,16,64,256]{3,2,1,0:T(8,128)(2,1)} %bitcast.10, bf16[256,3072]{1,0:T(8,128)(2,1)} %bitcast.9), custom_call_target="tpu_custom_call" | custom-call | tf_op jit(solution)/shard_map/pallas_call | solution.py:380
  74.3 1.3 %shard_map.77 = (bf16[2,16,64,256]{3,2,1,0:T(8,128)(2,1)}, bf16[256,1536]{1,0:T(8,128)(2,1)}, f32[2,8]{1,0:T(2,128)}) custom-call(bf16[2,16,64,256]{3,2,1,0:T(8,128)(2,1)S(1)} %get-tuple-element.9.dact_in, bf16[256,1536]{1,0:T(8,128)(2,1)S(1)} %get-tuple-element.10.dw_in, f32[2,8]{1,0:T(2,128)S(1)} %get-tuple-element.11.droute_in), custom_call_target="tpu_custom_call" | custom-call | tf_op jit(solution)/shard_map/pallas_call | solution.py:429

commit v3 on v2

--- a/solution.py
+++ b/solution.py
@@ -22,8 +22,8 @@
     tok_hbm, route_hbm, weight_hbm, act_hbm, w_hbm,
     dact, dw, droute,
     tok_ref, route_ref, weight_ref, act, w, wt, outgoing, zbuf, rows, hid, cgate, cup, hidt, drel, grad, grad_in,
-    last, last_in, psum, psum_in, colsum, colsum_in,
-    local_sem, zsend, zrecv, gsend, grecv, psend, precv, csend, crecv, xsend, xrecv,
+    last, last_in, psum, psum_in, colsum, colsum_in, late_in,
+    local_sem, zsend, zrecv, gsend, grecv, psend, precv, csend, crecv, lsend, lrecv, xsend, xrecv, far_sem,
 ):
     e = lax.axis_index("expert")
     t = lax.axis_index("etp")
@@ -50,10 +50,14 @@
     load_act, load_w = loads[3:]
 
     barrier = pltpu.get_barrier_semaphore()
-    for k in range(1, 16):
-        pl.semaphore_signal(barrier, inc=1, device_id=at(x, y, (z + k) % 16), device_id_type=MESH)
-        pl.semaphore_signal(barrier, inc=1, device_id=at_col((col + k) % 16), device_id_type=MESH)
-    pl.semaphore_signal(barrier, inc=1, device_id=sibling, device_id_type=MESH)
+    near = [at(x, y, (z + k) % 16) for k in (1, 15, 2, 14)]
+    near += [at((x + k) % 4, y, z) for k in (1, 3, 2)] + [at(x, (y + k) % 4, z) for k in (1, 3, 2)] + [sibling]
+    for device in near:
+        pl.semaphore_signal(barrier, inc=1, device_id=device, device_id_type=MESH)
+
+    def tell(i):
+        for k in (2 << i, 16 - (2 << i)):
+            pl.semaphore_signal(far_sem.at[i], inc=1, device_id=at(x, y, (z + k) % 16), device_id_type=MESH)
 
     spread = (iota((8, 128), 1) % 8 == iota((8, 128), 0)).astype(BF16)
     for k in range(3):
@@ -74,7 +78,7 @@
     slots = jnp.dot(pick[:, 0:32], folded.astype(BF16), preferred_element_type=F32)
     outgoing[...] = slots.astype(BF16).reshape(8, 16, FOLD)
 
-    pl.semaphore_wait(barrier, 31)
+    pl.semaphore_wait(barrier, len(near))
 
     sends = []
 
@@ -95,7 +99,7 @@
             sends.append(copy)
 
     along(0)
-    along(1)
+    tell(0)
     zbuf[0, 0] = outgoing[e]
 
     mrow, mcol = iota((64, 64), 0), iota((64, 64), 1)
@@ -230,25 +234,27 @@
 
             second_product(j, half, store)
 
-    def to_columns(js):
+    early = pl.ds(0, 2)
+
+    def to_columns():
         for k in range(1, 16):
             cc = (col + k) % 16
             copy = pltpu.make_async_remote_copy(
-                src_ref=psum.at[cc // 8, js],
-                dst_ref=psum_in.at[col, js],
-                send_sem=psend.at[js.start // 3, k - 1],
-                recv_sem=precv.at[js.start // 3],
+                src_ref=psum.at[cc // 8, early],
+                dst_ref=psum_in.at[col],
+                send_sem=psend.at[k - 1],
+                recv_sem=precv,
                 device_id=at_col(cc),
                 device_id_type=MESH,
             )
             copy.start()
             sends.append(copy)
-        psum_in[col, js] = psum[col // 8, js]
-
-    def along_column(js):
-        arrived = psum_in.at[pl.ds(0, 15), js]
-        pltpu.make_async_copy(arrived, arrived, precv.at[js.start // 3]).wait()
-        for j in range(js.start, js.start + js.size):
+        psum_in[col] = psum[col // 8, early]
+
+    def along_column():
+        arrived = psum_in.at[pl.ds(0, 15)]
+        pltpu.make_async_copy(arrived, arrived, precv).wait()
+        for j in range(2):
             total = jnp.sum(psum_in[:, j], axis=0)
             for k, near in enumerate(NEAR[j]):
                 turned = total if k == 0 else jnp.concatenate([total[:, 4 * k :], total[:, : 4 * k]], axis=1)
@@ -267,12 +273,34 @@
                 copy.start()
                 sends.append(copy)
 
+    def to_tokens(j):
+        for i in range(16):
+            cc = (col + 15 - i) % 16
+            for k, near in enumerate(NEAR[j]):
+                copy = pltpu.make_async_remote_copy(
+                    src_ref=psum.at[cc // 8, j],
+                    dst_ref=late_in.at[j - 2, k, col],
+                    send_sem=lsend.at[j - 2],
+                    recv_sem=lrecv.at[j - 2],
+                    device_id=(
+                        (z + near) % 8,
+                        (cc // 4) * 8 + (cc % 4) * 2 + ((z + near) % 16) // 8,
+                        p,
+                    ),
+                    device_id_type=MESH,
+                )
+                copy.start()
+
     def landed(copies):
         for copy in copies:
             copy.wait_recv()
 
+    pl.semaphore_wait(far_sem.at[0], 2)
+    tell(1)
+    along(1)
     assemble(0)
     a0 = one(0)
+    pl.semaphore_wait(far_sem.at[1], 2)
     along(2)
     along(3)
     load_act.wait()
@@ -299,10 +327,13 @@
     c2 = onward(2, b2)
     landed(c1)
     compute(1)
+    to_columns()
     b3 = two(3, a3)
     landed(c2)
     compute(2)
     c3 = onward(3, b3)
+    to_tokens(2)
+    along_column()
 
     def to_sibling(i, src, dst):
         copy = pltpu.make_async_remote_copy(
@@ -312,14 +343,14 @@
         sends.append(copy)
         return copy
 
-    for copy in sends[:-22]:
+    under_way = len(sends) - 18 - 15 - 7
+    for copy in sends[:under_way]:
         copy.wait_send()
-    sends = sends[-22:]
+    sends = sends[under_way:]
     most = to_sibling(0, grad.at[1 - p], grad_in)
-    to_columns(pl.ds(0, 3))
     landed(c3)
     d_out = first_product(3)
-    to_columns(pl.ds(3, 1))
+    to_tokens(3)
 
     def store_last(cols, term):
         last[:, cols] = term.astype(BF16)
@@ -329,9 +360,7 @@
 
     second_product(3, 1 - p, store_last)
     rest = to_sibling(1, last, last_in)
-    along_column(pl.ds(0, 3))
     slopes(3, d_out)
-    along_column(pl.ds(3, 1))
     second_product(3, p, store_grad)
     for i in range(2):
         for c in range(16):
@@ -342,8 +371,15 @@
     for k in range(3):
         cols = slice(k * 512, (k + 1) * 512)
         dw[:, cols] = (grad[p, :, cols] + grad_in[:, cols] + last_in[:, cols].astype(F32)).astype(BF16)
-    arrived = colsum_in.at[pl.ds(0, 15)]
+    arrived = colsum_in.at[pl.ds(0, 7)]
     pltpu.make_async_copy(arrived, arrived, crecv).wait()
+    for j in (2, 3):
+        late = late_in.at[j - 2]
+        pltpu.make_async_copy(late, late, lrecv.at[j - 2]).wait()
+        for k, near in enumerate(NEAR[j]):
+            total = jnp.sum(late_in[j - 2, k], axis=0)
+            turned = total if k == 0 else jnp.concatenate([total[:, 4 * k :], total[:, : 4 * k]], axis=1)
+            colsum_in[(z + 16 - near) % 16] = turned
     value = jnp.zeros((128, 128), F32)
     for i in range(8):
         both = colsum_in[i] + colsum_in[i + 8]
@@ -356,6 +392,8 @@
         droute[k : k + 1, :] = score[:, 0:8]
     for copy in sends:
         copy.wait_send()
+    for i in range(2):
+        pltpu.make_async_copy(late_in.at[i], late_in.at[i], lsend.at[i]).wait()
 
 
 def finish(dact_in, dw_in, droute_in, dact, dw, droute, sem):
@@ -402,20 +440,24 @@
             pltpu.VMEM((256, HALF), BF16),
             pltpu.VMEM((256, HALF), BF16),
             pltpu.VMEM((2, 4, 1, 128), F32),
-            pltpu.VMEM((16, 4, 1, 128), F32),
-            pltpu.VMEM((4, 4, 1, 128), F32),
+            pltpu.VMEM((16, 2, 1, 128), F32),
+            pltpu.VMEM((2, 4, 1, 128), F32),
             pltpu.VMEM((16, 1, 128), F32),
+            pltpu.VMEM((2, 4, 16, 1, 128), F32),
             dma((5,)),
             dma((4, 4)),
             dma((4,)),
             dma((4, 18)),
             dma((4, 18)),
-            dma((2, 15)),
-            dma((2,)),
-            dma((4, 4)),
+            dma((15,)),
+            dma,
+            dma((2, 4)),
             dma,
             dma((2,)),
             dma((2,)),
+            dma((2,)),
+            dma((2,)),
+            pltpu.SemaphoreType.REGULAR((2,)),
         ],
         compiler_params=pltpu.CompilerParams(
             collective_id=0, has_side_effects=True, vmem_limit_bytes=40 * 1024 * 1024

time: 75.7 us -> 73.4 us (0.970)
  the two profiles are of different devices: /device:TPU:2 before, /device:TPU:64 now
where the time goes in v3:
time: 73.4 us; the launch traced here: 73.3 us
  Pallas kernels  72.7 us (99%)
    pallas_call x1, Pallas kernels, per_device(): pl.pallas_call(kernel, out_shape=shapes, in_specs=[hbm] * 5, out_specs=(p...  71.4 us

profile of v3, /device:TPU:64, one launch (start us, length us, event | category | flops | bytes accessed | tf_op | source)
XLA Modules:
  0.0 73.3 jit_solution(14965193147938451445)
XLA Ops:
  0.6 71.4 %shard_map.76 = (bf16[2,16,64,256]{3,2,1,0:T(8,128)(2,1)S(1)}, bf16[256,1536]{1,0:T(8,128)(2,1)S(1)}, f32[2,8]{1,0:T(2,128)S(1)}) custom-call(bf16[8,3072]{1,0:T(8,128)(2,1)} %tok_hbm.1, s32[2,8]{1,0:T(2,128)} %bitcast.11, bf16[2,8]{1,0:T(2,128)(2,1)} %bitcast.12, bf16[2,16,64,256]{3,2,1,0:T(8,128)(2,1)} %bitcast.10, bf16[256,3072]{1,0:T(8,128)(2,1)} %bitcast.9), custom_call_target="tpu_custom_call" | custom-call | tf_op jit(solution)/shard_map/pallas_call | solution.py:418
  72.0 1.3 %shard_map.77 = (bf16[2,16,64,256]{3,2,1,0:T(8,128)(2,1)}, bf16[256,1536]{1,0:T(8,128)(2,1)}, f32[2,8]{1,0:T(2,128)}) custom-call(bf16[2,16,64,256]{3,2,1,0:T(8,128)(2,1)S(1)} %get-tuple-element.9.dact_in, bf16[256,1536]{1,0:T(8,128)(2,1)S(1)} %get-tuple-element.10.dw_in, f32[2,8]{1,0:T(2,128)S(1)} %get-tuple-element.11.droute_in), custom_call_target="tpu_custom_call" | custom-call | tf_op jit(solution)/shard_map/pallas_call | solution.py:471

commit v4 on v3

--- a/solution.py
+++ b/solution.py
@@ -11,6 +11,7 @@
 D = 3072
 HALF = D // 2
 FOLD = D // 4
+STEP = HALF // 4
 NEAR = ((0, 1, 15, 2), (14, 13, 3, 4), (12, 11, 5, 6), (10, 9, 7, 8))
 
 
@@ -21,7 +22,7 @@
 def kernel(
     tok_hbm, route_hbm, weight_hbm, act_hbm, w_hbm,
     dact, dw, droute,
-    tok_ref, route_ref, weight_ref, act, w, wt, outgoing, zbuf, rows, hid, cgate, cup, hidt, drel, grad, grad_in,
+    tok_ref, route_ref, weight_ref, act, w, wt, outgoing, fold, zbuf, rows, hid, cgate, cup, hidt, drel, grad, grad_in,
     last, last_in, psum, psum_in, colsum, colsum_in, late_in,
     local_sem, zsend, zrecv, gsend, grecv, psend, precv, csend, crecv, lsend, lrecv, xsend, xrecv, far_sem,
 ):
@@ -74,7 +75,13 @@
     hit = jnp.logical_and(hit, (row // 4) % 4 == lane // 8)
     pick = jnp.where(hit, jnp.where(first, gates[0:1], gates[1:2]), 0.0).astype(BF16)
     token = tok_ref[...].astype(F32)
-    folded = jnp.concatenate([token[:, i * FOLD : (i + 1) * FOLD] for i in range(4)], axis=0)
+    folded = jnp.concatenate(
+        [
+            jnp.concatenate([token[:, h * HALF + i * STEP : h * HALF + (i + 1) * STEP] for h in range(2)], axis=1)
+            for i in range(4)
+        ],
+        axis=0,
+    )
     slots = jnp.dot(pick[:, 0:32], folded.astype(BF16), preferred_element_type=F32)
     outgoing[...] = slots.astype(BF16).reshape(8, 16, FOLD)
 
@@ -89,7 +96,7 @@
             zz = (z + 16 - near) % 16
             copy = pltpu.make_async_remote_copy(
                 src_ref=outgoing.at[zz % 8],
-                dst_ref=zbuf.at[j, k],
+                dst_ref=fold.at[x, y, k] if j == 0 else zbuf.at[j, k],
                 send_sem=zsend.at[j, k],
                 recv_sem=zrecv.at[j],
                 device_id=at(x, y, zz),
@@ -100,21 +107,32 @@
 
     along(0)
     tell(0)
-    zbuf[0, 0] = outgoing[e]
+    fold[x, y, 0] = outgoing[e]
 
     mrow, mcol = iota((64, 64), 0), iota((64, 64), 1)
     unfold = jnp.logical_and(mrow // 16 == (mcol // 4) % 4, (mrow // 4) % 4 == mcol // 16)
     unfold = jnp.logical_and(unfold, mrow % 4 == mcol % 4).astype(F32).astype(BF16)
 
+    def unfolded(block, j, xx, yy):
+        flat = jnp.dot(unfold, block.reshape(64, FOLD), preferred_element_type=F32).astype(BF16)
+        for h in range(2):
+            for i in range(4):
+                cols = slice(h * HALF + i * STEP, h * HALF + (i + 1) * STEP)
+                rows[j, xx, yy, :, cols] = flat[i * 16 : (i + 1) * 16, h * STEP : (h + 1) * STEP]
+
+    def arrive(j):
+        landed = fold.at[x, y, pl.ds(1, 3)] if j == 0 else zbuf.at[j]
+        pltpu.make_async_copy(landed, landed, zrecv.at[j]).wait()
+
     def assemble(j):
-        landed = zbuf.at[j, pl.ds(1, 3)] if j == 0 else zbuf.at[j]
-        pltpu.make_async_copy(landed, landed, zrecv.at[j]).wait()
-        block = zbuf[j].reshape(64, FOLD)
-        flat = jnp.dot(unfold, block, preferred_element_type=F32).astype(BF16)
-        for i in range(4):
-            rows[j, x, y, :, i * FOLD : (i + 1) * FOLD] = flat[i * 16 : (i + 1) * 16]
-
-    every = pl.ds(0, 4)
+        arrive(j)
+        unfolded(zbuf[j], j, x, y)
+
+    def assemble_near():
+        @pl.loop(0, 16)
+        def _(c):
+            unfolded(fold[c // 4, c % 4], 0, c // 4, c % 4)
+
     whole = (pl.ds(0, HALF), pl.ds(HALF, HALF))
     part = (
         (pl.ds(0, FOLD), pl.ds(FOLD, FOLD)),
@@ -137,37 +155,43 @@
     right, left = (at(xr, y, z), at(x, yr, z)), (at(xl, y, z), at(x, yl, z))
     across = (at((x + 2) % 4, y, z), at(x, (y + 2) % 4, z))
 
-    def line(j, half, xx, yy, columns):
-        return rows.at[j, xx, yy, :, columns]
-
-    def one(j):
+    def line(unit, h, xx, yy):
+        if unit < 2:
+            return fold.at[xx, yy, pl.ds(unit, 1 + 2 * unit), :, pl.ds(h * STEP, STEP)]
+        return rows.at[unit - 1, xx, yy, :, whole[h]]
+
+    def piece(unit, h, at_line, i):
+        if unit < 2:
+            both = pl.ds(2 * i, 2)
+            return line(unit, h, *((both, at_line) if h == 0 else (at_line, both)))
+        both = pl.ds(0, 4)
+        return rows.at[unit - 1, *((both, at_line) if h == 0 else (at_line, both)), :, part[h][i]]
+
+    def one(unit):
         copies = []
         for d, target in enumerate((across, right, left)):
             for h in range(2):
-                copies.append(push(j, 9 * h + d, line(j, h, x, y, whole[h]), target[h]))
+                copies.append(push(unit, 9 * h + d, line(unit, h, x, y), target[h]))
         return copies
 
-    def two(j, got):
+    def two(unit, got):
         for copy in got:
             copy.wait_recv()
         copies = []
         for i in range(2):
             for d in range(2):
                 for h in range(2):
-                    xx, yy = (every, y) if h == 0 else (x, every)
-                    ref = line(j, h, xx, yy, part[h][d if i == 0 else 1 - d])
-                    copies.append(push(j, 9 * h + 3 + 2 * i + d, ref, (right, left)[d][1 - h]))
+                    ref = piece(unit, h, (y, x)[h], d if i == 0 else 1 - d)
+                    copies.append(push(unit, 9 * h + 3 + 2 * i + d, ref, (right, left)[d][1 - h]))
         return copies
 
-    def onward(j, got):
+    def onward(unit, got):
         copies = []
         for d in range(2):
             for h in range(2):
                 got[2 * d + h].wait_recv()
-                side = ((xl, yl), (xr, yr))[d]
-                xx, yy = (every, side[1]) if h == 0 else (side[0], every)
-                ref = line(j, h, xx, yy, part[h][d])
-                copies.append(push(j, 9 * h + 7 + d, ref, (right, left)[d][1 - h]))
+                side = ((yl, xl), (yr, xr))[d][h]
+                copies.append(push(unit, 9 * h + 7 + d, piece(unit, h, side, d), (right, left)[d][1 - h]))
         return copies + got[4:]
 
     frow, fcol = iota((64, 64), 0), iota((64, 64), 1)
@@ -274,8 +298,8 @@
                 sends.append(copy)
 
     def to_tokens(j):
-        for i in range(16):
-            cc = (col + 15 - i) % 16
+        for i in (10, 11, 9, 14, 6, 15, 13, 7, 5, 8, 2, 12, 4, 3, 1, 0):
+            cc = ((x + i // 4) % 4) * 4 + (y + i % 4) % 4
             for k, near in enumerate(NEAR[j]):
                 copy = pltpu.make_async_remote_copy(
                     src_ref=psum.at[cc // 8, j],
@@ -295,43 +319,48 @@
         for copy in copies:
             copy.wait_recv()
 
+    am = one(0)
     pl.semaphore_wait(far_sem.at[0], 2)
     tell(1)
     along(1)
-    assemble(0)
-    a0 = one(0)
+    bm = two(0, am)
+    arrive(0)
+    a0 = one(1)
+    cm = onward(0, bm)
     pl.semaphore_wait(far_sem.at[1], 2)
     along(2)
     along(3)
     load_act.wait()
     prepare(0)
+    b0 = two(1, a0)
+    assemble(1)
+    a1 = one(2)
     prepare(1)
-    b0 = two(0, a0)
-    assemble(1)
-    a1 = one(1)
+    c0 = onward(1, b0)
     prepare(2)
-    c0 = onward(0, b0)
+    b1 = two(2, a1)
     prepare(3)
-    b1 = two(1, a1)
     load_w.wait()
     transpose_w()
     flip()
     assemble(2)
-    a2 = one(2)
-    c1 = onward(1, b1)
+    a2 = one(3)
+    c1 = onward(2, b1)
+    landed(cm)
     landed(c0)
+    assemble_near()
     compute(0)
-    b2 = two(2, a2)
+    b2 = two(3, a2)
     assemble(3)
-    a3 = one(3)
-    c2 = onward(2, b2)
+    a3 = one(4)
+    c2 = onward(3, b2)
     landed(c1)
     compute(1)
     to_columns()
-    b3 = two(3, a3)
+    b3 = two(4, a3)
     landed(c2)
     compute(2)
-    c3 = onward(3, b3)
+    c3 = onward(4, b3)
     to_tokens(2)
     along_column()
 
@@ -428,6 +457,7 @@
             pltpu.VMEM((256, D), BF16),
             pltpu.VMEM((D, 256), BF16),
             pltpu.VMEM((8, 16, FOLD), BF16),
+            pltpu.VMEM((4, 4, 4, 16, FOLD), BF16),
             pltpu.VMEM((4, 4, 16, FOLD), BF16),
             pltpu.VMEM((4, 4, 4, 16, D), BF16),
             pltpu.VMEM((4, 256, 256), F32),
@@ -447,8 +477,8 @@
             dma((5,)),
             dma((4, 4)),
             dma((4,)),
-            dma((4, 18)),
-            dma((4, 18)),
+            dma((5, 18)),
+            dma((5, 18)),
             dma((15,)),
             dma,
             dma((2, 4)),

time: 73.4 us -> 71.4 us (0.973)
  Pallas kernels: 72.7 us -> 70.6 us
    pallas_call x1, Pallas kernels: 71.4 us -> 69.3 us  [per_device(): pl.pallas_call(kernel, out_shape=shapes, in_specs=[hbm] * 5, out_specs=(p...]
where the time goes in v4:
time: 71.4 us; the launch traced here: 71.3 us
  Pallas kernels  70.6 us (99%)
    pallas_call x1, Pallas kernels, per_device(): pl.pallas_call(kernel, out_shape=shapes, in_specs=[hbm] * 5, out_specs=(p...  69.3 us

profile of v4, /device:TPU:64, one launch (start us, length us, event | category | flops | bytes accessed | tf_op | source)
XLA Modules:
  0.0 71.3 jit_solution(12144730923410720036)
XLA Ops:
  0.6 69.3 %shard_map.76 = (bf16[2,16,64,256]{3,2,1,0:T(8,128)(2,1)S(1)}, bf16[256,1536]{1,0:T(8,128)(2,1)S(1)}, f32[2,8]{1,0:T(2,128)S(1)}) custom-call(bf16[8,3072]{1,0:T(8,128)(2,1)} %tok_hbm.1, s32[2,8]{1,0:T(2,128)} %bitcast.11, bf16[2,8]{1,0:T(2,128)(2,1)} %bitcast.12, bf16[2,16,64,256]{3,2,1,0:T(8,128)(2,1)} %bitcast.10, bf16[256,3072]{1,0:T(8,128)(2,1)} %bitcast.9), custom_call_target="tpu_custom_call" | custom-call | tf_op jit(solution)/shard_map/pallas_call | solution.py:447
  70.0 1.3 %shard_map.77 = (bf16[2,16,64,256]{3,2,1,0:T(8,128)(2,1)}, bf16[256,1536]{1,0:T(8,128)(2,1)}, f32[2,8]{1,0:T(2,128)}) custom-call(bf16[2,16,64,256]{3,2,1,0:T(8,128)(2,1)S(1)} %get-tuple-element.9.dact_in, bf16[256,1536]{1,0:T(8,128)(2,1)S(1)} %get-tuple-element.10.dw_in, f32[2,8]{1,0:T(2,128)S(1)} %get-tuple-element.11.droute_in), custom_call_target="tpu_custom_call" | custom-call | tf_op jit(solution)/shard_map/pallas_call | solution.py:501

commit v5 on v4

--- a/solution.py
+++ b/solution.py
@@ -340,24 +340,24 @@
     prepare(2)
     b1 = two(2, a1)
     prepare(3)
+    assemble(2)
+    a2 = one(3)
+    c1 = onward(2, b1)
     load_w.wait()
     transpose_w()
     flip()
-    assemble(2)
-    a2 = one(3)
-    c1 = onward(2, b1)
+    b2 = two(3, a2)
+    assemble(3)
+    a3 = one(4)
     landed(cm)
     landed(c0)
     assemble_near()
     compute(0)
-    b2 = two(3, a2)
-    assemble(3)
-    a3 = one(4)
     c2 = onward(3, b2)
+    b3 = two(4, a3)
     landed(c1)
     compute(1)
     to_columns()
-    b3 = two(4, a3)
     landed(c2)
     compute(2)
     c3 = onward(4, b3)

time: 71.4 us -> 71.3 us (level)
  no operation moved by 1% of the time
where the time goes in v5:
time: 71.3 us; the launch traced here: 71.1 us
  Pallas kernels  70.5 us (99%)
    pallas_call x1, Pallas kernels, per_device(): pl.pallas_call(kernel, out_shape=shapes, in_specs=[hbm] * 5, out_specs=(p...  69.2 us

profile of v5, /device:TPU:64, one launch (start us, length us, event | category | flops | bytes accessed | tf_op | source)
XLA Modules:
  0.0 71.1 jit_solution(13107196044149218098)
XLA Ops:
  0.6 69.2 %shard_map.76 = (bf16[2,16,64,256]{3,2,1,0:T(8,128)(2,1)S(1)}, bf16[256,1536]{1,0:T(8,128)(2,1)S(1)}, f32[2,8]{1,0:T(2,128)S(1)}) custom-call(bf16[8,3072]{1,0:T(8,128)(2,1)} %tok_hbm.1, s32[2,8]{1,0:T(2,128)} %bitcast.11, bf16[2,8]{1,0:T(2,128)(2,1)} %bitcast.12, bf16[2,16,64,256]{3,2,1,0:T(8,128)(2,1)} %bitcast.10, bf16[256,3072]{1,0:T(8,128)(2,1)} %bitcast.9), custom_call_target="tpu_custom_call" | custom-call | tf_op jit(solution)/shard_map/pallas_call | solution.py:447
  69.9 1.3 %shard_map.77 = (bf16[2,16,64,256]{3,2,1,0:T(8,128)(2,1)}, bf16[256,1536]{1,0:T(8,128)(2,1)}, f32[2,8]{1,0:T(2,128)}) custom-call(bf16[2,16,64,256]{3,2,1,0:T(8,128)(2,1)S(1)} %get-tuple-element.9.dact_in, bf16[256,1536]{1,0:T(8,128)(2,1)S(1)} %get-tuple-element.10.dw_in, f32[2,8]{1,0:T(2,128)S(1)} %get-tuple-element.11.droute_in), custom_call_target="tpu_custom_call" | custom-call | tf_op jit(solution)/shard_map/pallas_call | solution.py:501
